TPU v7x, 256 devices: a whole 4x4x8 slice. The times are simulated.
256 devices in a mesh: grp: 8 (over x, core), dev: 32 (over z, y).
Axes of the slice: x: 4, y: 4, z: 8, core: 2. Of those that a mesh axis runs over, the one named last changes fastest.
Arguments:
- gap_field: float32 [1024, 768], P(('grp', 'dev')), may hold values from -6 to 6
- precond_weight: float32 [1024, 768], P(('grp', 'dev')), may hold values from 0.5 to 4
- slab_links: int32 [128, 4], P('dev'), may hold values from 0 to 127, as said below
- face_lengths: int32 [128, 4], P('dev'), may hold values from 64 to 128, as said below
- schur_inv: float32 [1024, 768, 768], P(('grp', 'dev')), may hold values from -40 to 40
- corner_map: int32 [1024, 24], P(('grp', 'dev')), may hold values from 0 to 3071
- corner_coupling: float32 [1024, 24, 768], P(('grp', 'dev')), may hold values from -0.21875 to 0.21875
- coarse_inv: float32 [3072, 3072], P('dev'), may hold values from -20 to 20, as said below
Outputs:
- multipliers: float32 [1024, 768], P(('grp', 'dev'))
- residual: float32 [1024, 768], P(('grp', 'dev'))
Inputs may be any that keep to these rules, and one draw needn't show every extreme that they name: slab_links is a symmetric neighbour relation of a periodic two-dimensional grid of slab positions: position slab_links[p, 0] has p as its -a neighbour and slab_links[p, 1] has p as its +a neighbour (likewise columns 2 and 3 for b). Position p lies on device p // 4; the +a neighbours of all positions of one device lie on one other device, the -a neighbours on a third one, and the b neighbours on the device itself. `face_lengths`: the live length of a face equals that of the matching face across the interface; some face is fully live. coarse_inv is symmetric.
All inputs are finite; a program needn't handle non-finite values.
Results may differ from a plain program's by a relative error of at most 0.0003.
Values sent between devices are 32-bit elements; how exact they have to be, the bound alone decides.
A program may use at most 64 MiB of HBM per device.

v0:
```python
import jax
import jax.numpy as jnp
from jax import lax
from jax.sharding import PartitionSpec as P

ITERS = 3


highest = lax.Precision.HIGHEST


def from_behind(value, axis, by):
    length = lax.axis_size(axis)
    return lax.ppermute(value, axis, [(i, (i + by) % length) for i in range(length)])


def residual_norm(residual, scaled):
    return lax.psum(0.5 * jnp.sum(residual * scaled), ("grp", "dev"))


def per_device(
    gap_field,
    precond_weight,
    slab_links,
    face_lengths,
    schur_inv,
    corner_map,
    corner_coupling,
    coarse_inv,
):
    subdomains = gap_field.shape[0]
    face_width = gap_field.shape[1] // 6
    corner_count = corner_map.shape[1]
    coarse_width = coarse_inv.shape[1]
    group_size = lax.axis_size("dev")
    slab_count = group_size * subdomains
    face_sign = jnp.array([1.0, -1.0, 1.0, -1.0, 1.0, -1.0], jnp.float32)[:, None]
    live_slab = (
        jnp.arange(face_width, dtype=jnp.int32)[None, None, :] < face_lengths[:, :, None]
    ).astype(jnp.float32)
    face_mask = jnp.concatenate(
        [jnp.ones((subdomains, 2, face_width), jnp.float32), live_slab], axis=1
    )
    targets = (
        slab_links[:, 0:2, None] == jnp.arange(slab_count, dtype=jnp.int32)[None, None, :]
    ).astype(jnp.float32)
    beside_slots = (
        slab_links[:, 2:4, None] % subdomains
        == jnp.arange(subdomains, dtype=jnp.int32)[None, None, :]
    ).astype(jnp.float32)
    corner_pick = (
        corner_map.reshape(-1)[:, None] == jnp.arange(coarse_width, dtype=jnp.int32)[None, :]
    ).astype(jnp.float32)

    def opposite(values):
        upper_face = from_behind(values[:, 1].reshape(-1), "grp", -1).reshape(
            subdomains, face_width
        )
        lower_face = from_behind(values[:, 0].reshape(-1), "grp", 1).reshape(subdomains, face_width)
        paired = lax.all_gather(
            values[:, 2:4].reshape(subdomains, 2 * face_width), "dev", axis=0, tiled=True
        )
        plus_side = jnp.dot(targets[:, 0], paired[:, face_width:], precision=highest)
        minus_side = jnp.dot(targets[:, 1], paired[:, :face_width], precision=highest)
        beside_plus = jnp.dot(beside_slots[:, 0], values[:, 5], precision=highest)
        beside_minus = jnp.dot(beside_slots[:, 1], values[:, 4], precision=highest)
        return jnp.stack(
            [upper_face, lower_face, plus_side, minus_side, beside_plus, beside_minus], axis=1
        )

    def interface_jump(values):
        return face_mask * face_sign * (values - opposite(values))

    weights = precond_weight.reshape(subdomains, 6, face_width)
    scaling = weights + opposite(weights)
    residual = interface_jump(gap_field.reshape(subdomains, 6, face_width))
    scaled = scaling * residual
    direction = scaled
    norm_now = residual_norm(residual, scaled)
    solution = jnp.zeros_like(residual)
    iterations = ITERS
    for iteration in range(iterations):
        face_load = (face_sign * direction).reshape(subdomains, 6 * face_width)
        response = jnp.einsum("sij,sj->si", schur_inv, face_load, precision=highest)
        corner_load = jnp.einsum("skj,sj->sk", corner_coupling, face_load, precision=highest)
        operator_local_rhs = jnp.dot(corner_load.reshape(-1), corner_pick, precision=highest)
        coarse_rhs = lax.psum(operator_local_rhs, ("grp", "dev"))
        row_part = jnp.dot(coarse_inv, coarse_rhs, precision=highest)
        coarse_sol = lax.all_gather(row_part, "dev", axis=0, tiled=True)
        corner_values = jnp.dot(corner_pick, coarse_sol, precision=highest).reshape(
            subdomains, corner_count
        )
        response = response + jnp.einsum(
            "skj,sk->sj", corner_coupling, corner_values, precision=highest
        )
        image = interface_jump(response.reshape(subdomains, 6, face_width))
        curvature_sum = lax.psum(0.5 * jnp.sum(direction * image), ("grp", "dev"))
        step_size = norm_now / curvature_sum
        solution = solution + step_size * direction
        residual = residual - step_size * image
        if iteration + 1 < iterations:
            scaled = scaling * residual
            norm_next = residual_norm(residual, scaled)
            direction = scaled + norm_next / norm_now * direction
            norm_now = norm_next
    return (
        solution.reshape(subdomains, 6 * face_width),
        residual.reshape(subdomains, 6 * face_width),
    )


def solution(mesh):
    return jax.shard_map(
        per_device,
        mesh=mesh,
        in_specs=(
            P(("grp", "dev"), None),
            P(("grp", "dev"), None),
            P("dev", None),
            P("dev", None),
            P(("grp", "dev"), None, None),
            P(("grp", "dev"), None),
            P(("grp", "dev"), None, None),
            P("dev", None),
        ),
        out_specs=(P(("grp", "dev"), None), P(("grp", "dev"), None)),
        check_vma=False,
    )
```

profile of v0, /device:TPU:1, one launch (start us, length us, event | category | flops | bytes accessed | tf_op | source)
XLA Modules:
  0.0 1306.7 jit_solution(5868862362272150230)
XLA Ops:
  0.7 0.8 slice_bitcast_fusion.27
  1.5 3.2 collective-permute-start.2
  4.7 0.7 slice_bitcast_fusion.33
  5.4 0.5 collective-permute-start
  5.9 1.2 collective-permute-start.1
  7.2 0.7 slice_bitcast_fusion.3
  7.9 0.7 slice_bitcast_fusion.4
  8.6 0.8 add_select_fusion
  9.6 35.8 %all-gather.1 = f32[32,4,256]{2,1,0:T(4,128)S(1)} all-gather(f32[1,4,256]{2,1,0:T(4,128)S(1)} %slice_bitcast_fusion.3), channel_id=1, replica_groups=mesh['grp'=8,'dev'=32] {'dev'}, dimensions={0}, use_global_device_ids=true | all-gather | bytes 135168 | tf_op jit(solution)/shard_map/all_gather | solution.py:60
  45.6 0.8 copy.16
  46.4 32.7 %all-gather = f32[32,4,256]{2,1,0:T(4,128)S(1)} all-gather(f32[1,4,256]{2,1,0:T(4,128)S(1)} %slice_bitcast_fusion.4), channel_id=1, replica_groups=mesh['grp'=8,'dev'=32] {'dev'}, dimensions={0}, use_global_device_ids=true | all-gather | bytes 135168 | tf_op jit(solution)/shard_map/all_gather | solution.py:60
  79.2 0.8 eq.49
  80.0 1.3 dynamic-slice
  82.3 0.8 fusion.19
  83.1 0.8 fusion.18
  84.6 0.4 fusion.56
  85.1 0.6 fusion.5
  85.6 94.5 %psum.64 = f32[3072]{0:T(1024)S(1)} all-reduce(f32[3072]{0:T(1024)S(1)} %bitcast.349), channel_id=1, replica_groups=mesh['grp'=8,'dev'=32] {'grp','dev'}, use_global_device_ids=true, to_apply=%region_2.3 | all-reduce | flops 3072 | bytes 24576 | tf_op jit(solution)/shard_map/psum | solution.py:87
  180.1 1.0 convolution_bitcast_fusion.22
  181.2 0.2 dynamic-update-slice
  181.4 112.0 %all-reduce.1 = f32[3072]{0:T(1024)S(1)} all-reduce(f32[3072]{0:T(1024)S(1)} %dynamic-update-slice), channel_id=1, replica_groups=mesh['grp'=8,'dev'=32] {'dev'}, use_global_device_ids=true, to_apply=%add.1 | all-reduce | flops 3072 | bytes 24576
  293.4 0.7 fusion.26
  294.2 0.3 fusion.66
  294.5 9.9 fusion.58
  304.4 28.5 %collective-permute-start.4 = (f32[512]{0:T(512)S(1)}, f32[512]{0:T(512)S(1)}, u32[]{:S(2)}, u32[]{:S(2)}) collective-permute-start(f32[512]{0:T(512)S(1)} %get-tuple-element.21), channel_id=1, source_target_pairs={{0,224},{32,0},{64,32},{96,64},{128,96},{160,128},{192,160},{224,1... | collective-permute-start | bytes 6152 | tf_op jit(solution)/shard_map/ppermute | solution.py:14
  332.9 30.1 %all-gather.2 = f32[32,4,256]{2,1,0:T(4,128)S(1)} all-gather(f32[1,4,256]{2,1,0:T(4,128)S(1)} %slice_bitcast_fusion.2), channel_id=1, replica_groups=mesh['grp'=8,'dev'=32] {'dev'}, dimensions={0}, use_global_device_ids=true | all-gather | bytes 135168 | tf_op jit(solution)/shard_map/all_gather | solution.py:60
  363.1 9.7 collective-permute-start.5
  372.7 0.8 collective-permute-done.5
  374.1 0.8 multiply_reduce_fusion.4
  376.3 76.8 %all-reduce.4 = (f32[]{:T(128)}, f32[]{:T(128)}) all-reduce(f32[]{:T(128)S(6)} %mul.142, f32[]{:T(128)S(6)} %mul.146), channel_id=1, replica_groups=mesh['grp'=8,'dev'=32] {'grp','dev'}, use_global_device_ids=true, to_apply=%region_1.2 | all-reduce | flops 2 | bytes 16 | tf_op jit(solution)/shard_map/psum | solution.py:18
  454.5 0.8 multiply_reduce_fusion.3
  455.9 73.4 %psum.66 = f32[]{:T(128)} all-reduce(f32[]{:T(128)S(6)} %mul.152), channel_id=1, replica_groups=mesh['grp'=8,'dev'=32] {'grp','dev'}, use_global_device_ids=true, to_apply=%region_6.7 | all-reduce | flops 1 | bytes 8 | tf_op jit(solution)/shard_map/psum | solution.py:18
  530.8 0.4 fusion.52
  531.1 9.9 fusion.54
  541.1 0.5 fusion.3
  541.6 74.4 %psum.67 = f32[3072]{0:T(1024)S(1)} all-reduce(f32[3072]{0:T(1024)S(1)} %bitcast.351), channel_id=1, replica_groups=mesh['grp'=8,'dev'=32] {'grp','dev'}, use_global_device_ids=true, to_apply=%region_7.8 | all-reduce | flops 3072 | bytes 24576 | tf_op jit(solution)/shard_map/psum | solution.py:87
  616.0 1.0 convolution_bitcast_fusion.21
  617.0 0.2 dynamic-update-slice.1
  617.3 112.6 %all-reduce.2 = f32[3072]{0:T(1024)S(1)} all-reduce(f32[3072]{0:T(1024)S(1)} %dynamic-update-slice.1), channel_id=1, replica_groups=mesh['grp'=8,'dev'=32] {'dev'}, use_global_device_ids=true, to_apply=%add.2 | all-reduce | flops 3072 | bytes 24576
  729.9 0.7 fusion.27
  730.7 0.3 fusion.67
  731.0 28.5 %collective-permute-start.6 = (f32[512]{0:T(512)S(1)}, f32[512]{0:T(512)S(1)}, u32[]{:S(2)}, u32[]{:S(2)}) collective-permute-start(f32[512]{0:T(512)S(1)} %get-tuple-element.19), channel_id=1, source_target_pairs={{0,224},{32,0},{64,32},{96,64},{128,96},{160,128},{192,160},{224,1... | collective-permute-start | bytes 6152 | tf_op jit(solution)/shard_map/ppermute | solution.py:14
  759.5 30.1 %all-gather.3 = f32[32,4,256]{2,1,0:T(4,128)S(1)} all-gather(f32[1,4,256]{2,1,0:T(4,128)S(1)} %slice_bitcast_fusion.1), channel_id=1, replica_groups=mesh['grp'=8,'dev'=32] {'dev'}, dimensions={0}, use_global_device_ids=true | all-gather | bytes 135168 | tf_op jit(solution)/shard_map/all_gather | solution.py:60
  789.7 9.4 collective-permute-start.7
  799.1 1.1 collective-permute-done.7
  800.8 0.7 multiply_reduce_fusion.2
  802.1 76.8 %psum.68 = f32[]{:T(128)} all-reduce(f32[]{:T(128)S(6)} %mul.158), channel_id=1, replica_groups=mesh['grp'=8,'dev'=32] {'grp','dev'}, use_global_device_ids=true, to_apply=%region_9.10 | all-reduce | flops 1 | bytes 8 | tf_op jit(solution)/shard_map/psum | solution.py:97
  880.3 0.7 multiply_reduce_fusion.1
  881.6 73.4 %psum.69 = f32[]{:T(128)} all-reduce(f32[]{:T(128)S(6)} %mul.164), channel_id=1, replica_groups=mesh['grp'=8,'dev'=32] {'grp','dev'}, use_global_device_ids=true, to_apply=%region_11.12 | all-reduce | flops 1 | bytes 8 | tf_op jit(solution)/shard_map/psum | solution.py:18
  956.5 0.4 fusion.48
  956.8 9.9 fusion.50
  966.8 0.5 fusion.1
  967.4 74.3 %psum.70 = f32[3072]{0:T(1024)S(1)} all-reduce(f32[3072]{0:T(1024)S(1)} %bitcast.353), channel_id=1, replica_groups=mesh['grp'=8,'dev'=32] {'grp','dev'}, use_global_device_ids=true, to_apply=%region_12.13 | all-reduce | flops 3072 | bytes 24576 | tf_op jit(solution)/shard_map/psum | solution.py:87
  1041.7 1.0 convolution_bitcast_fusion.20
  1042.9 112.7 %all-reduce.3 = f32[3072]{0:T(1024)S(1)} all-reduce(f32[3072]{0:T(1024)S(1)} %dynamic-update-slice.2), channel_id=1, replica_groups=mesh['grp'=8,'dev'=32] {'dev'}, use_global_device_ids=true, to_apply=%add.3 | all-reduce | flops 3072 | bytes 24576
  1155.6 0.7 fusion.28
  1156.4 0.3 fusion.68
  1156.8 28.5 %collective-permute-start.8 = (f32[512]{0:T(512)S(1)}, f32[512]{0:T(512)S(1)}, u32[]{:S(2)}, u32[]{:S(2)}) collective-permute-start(f32[512]{0:T(512)S(1)} %get-tuple-element.17), channel_id=1, source_target_pairs={{0,224},{32,0},{64,32},{96,64},{128,96},{160,128},{192,160},{224,1... | collective-permute-start | bytes 6152 | tf_op jit(solution)/shard_map/ppermute | solution.py:14
  1185.3 30.1 %all-gather.4 = f32[32,4,256]{2,1,0:T(4,128)S(1)} all-gather(f32[1,4,256]{2,1,0:T(4,128)S(1)} %slice_bitcast_fusion), channel_id=1, replica_groups=mesh['grp'=8,'dev'=32] {'dev'}, dimensions={0}, use_global_device_ids=true | all-gather | bytes 135168 | tf_op jit(solution)/shard_map/all_gather | solution.py:60
  1215.4 9.3 collective-permute-start.9
  1224.8 1.2 collective-permute-done.9
  1226.5 0.7 multiply_reduce_fusion
  1227.9 76.8 %psum.71 = f32[]{:T(128)} all-reduce(f32[]{:T(128)S(6)} %mul.170), channel_id=1, replica_groups=mesh['grp'=8,'dev'=32] {'grp','dev'}, use_global_device_ids=true, to_apply=%region_14.15 | all-reduce | flops 1 | bytes 8 | tf_op jit(solution)/shard_map/psum | solution.py:97
  1306.0 0.7 subtract_bitcast_fusion
  (78 shorter events, 4.3 us)
Async XLA Ops:
  0.6 179.5 %copy-start = (f32[96,3072]{1,0:T(8,128)S(1)}, f32[96,3072]{1,0:T(8,128)}, u32[]{:S(2)}) copy-start(f32[96,3072]{1,0:T(8,128)} %param.16) | copy-start | bytes 3538948
  0.6 83.9 %copy-start.3 = (f32[6]{0:T(128)S(1)}, f32[6]{0:T(128)}, u32[]{:S(2)}) copy-start(f32[6]{0:T(128)} %constant.25.clone) | copy-start | bytes 76
  0.7 83.9 %copy-start.2 = (f32[4,768]{1,0:T(4,128)S(1)}, f32[4,768]{1,0:T(4,128)}, u32[]{:S(2)}) copy-start(f32[4,768]{1,0:T(4,128)} %param.10) | copy-start | bytes 36868
  0.7 83.6 %copy-start.4 = (f32[4,768]{1,0:T(4,128)S(1)}, f32[4,768]{1,0:T(4,128)}, u32[]{:S(2)}) copy-start(f32[4,768]{1,0:T(4,128)} %param.9) | copy-start | bytes 36868
  0.7 83.9 %copy-start.1 = (f32[4,24,768]{2,1,0:T(8,128)S(1)}, f32[4,24,768]{2,1,0:T(8,128)}, u32[]{:S(2)}) copy-start(f32[4,24,768]{2,1,0:T(8,128)} %param.15) | copy-start | bytes 884740
  1.5 80.4 %collective-permute-start.2 = (f32[512]{0:T(512)S(1)}, f32[512]{0:T(512)S(1)}, u32[]{:S(2)}, u32[]{:S(2)}) collective-permute-start(f32[512]{0:T(512)S(1)} %get-tuple-element.25), channel_id=1, source_target_pairs={{0,224},{32,0},{64,32},{96,64},{128,96},{160,128},{192,160},{224,1... | collective-permute-start | bytes 6152 | tf_op jit(solution)/shard_map/ppermute | solution.py:14
  4.7 77.2 %collective-permute-start.3 = (f32[512]{0:T(512)S(1)}, f32[512]{0:T(512)S(1)}, u32[]{:S(2)}, u32[]{:S(2)}) collective-permute-start(f32[512]{0:T(512)S(1)} %get-tuple-element.24), channel_id=1, source_target_pairs={{0,32},{32,64},{64,96},{96,128},{128,160},{160,192},{192,224},{224... | collective-permute-start | bytes 6152 | tf_op jit(solution)/shard_map/ppermute | solution.py:14
  5.4 78.5 %collective-permute-start = (f32[512]{0:T(512)S(1)}, f32[512]{0:T(512)S(1)}, u32[]{:S(2)}, u32[]{:S(2)}) collective-permute-start(f32[512]{0:T(512)S(1)} %get-tuple-element.23), channel_id=1, source_target_pairs={{0,224},{32,0},{64,32},{96,64},{128,96},{160,128},{192,160},{224,1... | collective-permute-start | bytes 6152 | tf_op jit(solution)/shard_map/ppermute | solution.py:14
  5.9 78.0 %collective-permute-start.1 = (f32[512]{0:T(512)S(1)}, f32[512]{0:T(512)S(1)}, u32[]{:S(2)}, u32[]{:S(2)}) collective-permute-start(f32[512]{0:T(512)S(1)} %get-tuple-element.22), channel_id=1, source_target_pairs={{0,32},{32,64},{64,96},{96,128},{128,160},{160,192},{192,224},{224... | collective-permute-start | bytes 6152 | tf_op jit(solution)/shard_map/ppermute | solution.py:14
  304.4 68.4 %collective-permute-start.4 = (f32[512]{0:T(512)S(1)}, f32[512]{0:T(512)S(1)}, u32[]{:S(2)}, u32[]{:S(2)}) collective-permute-start(f32[512]{0:T(512)S(1)} %get-tuple-element.21), channel_id=1, source_target_pairs={{0,224},{32,0},{64,32},{96,64},{128,96},{160,128},{192,160},{224,1... | collective-permute-start | bytes 6152 | tf_op jit(solution)/shard_map/ppermute | solution.py:14
  363.1 10.5 collective-permute-start.5
  731.0 68.1 %collective-permute-start.6 = (f32[512]{0:T(512)S(1)}, f32[512]{0:T(512)S(1)}, u32[]{:S(2)}, u32[]{:S(2)}) collective-permute-start(f32[512]{0:T(512)S(1)} %get-tuple-element.19), channel_id=1, source_target_pairs={{0,224},{32,0},{64,32},{96,64},{128,96},{160,128},{192,160},{224,1... | collective-permute-start | bytes 6152 | tf_op jit(solution)/shard_map/ppermute | solution.py:14
  789.7 10.5 collective-permute-start.7
  1156.8 68.0 %collective-permute-start.8 = (f32[512]{0:T(512)S(1)}, f32[512]{0:T(512)S(1)}, u32[]{:S(2)}, u32[]{:S(2)}) collective-permute-start(f32[512]{0:T(512)S(1)} %get-tuple-element.17), channel_id=1, source_target_pairs={{0,224},{32,0},{64,32},{96,64},{128,96},{160,128},{192,160},{224,1... | collective-permute-start | bytes 6152 | tf_op jit(solution)/shard_map/ppermute | solution.py:14
  1215.4 10.5 collective-permute-start.9
where the time goes:
time: 1310 us
  blocking collectives  1120 us (85%)
  starting transfers between devices  119 us (9%)
  matrix products  42.6 us (3%)
    unnamed x3, blocking collectives  337 us
    psum x3, blocking collectives, per_device(): coarse_rhs = lax.psum(operator_local_rhs, ('grp', 'dev'))  243 us
    psum x3, blocking collectives, residual_norm(): return lax.psum(0.5 * jnp.sum(residual * scaled), ('grp', 'dev'))  224 us
    all_gather x5, blocking collectives, opposite(): lax.all_gather(values[:, 2:4].reshape(subdomains, 2 * face_width), 'dev',...  159 us
    psum x2, blocking collectives, per_device(): curvature_sum = lax.psum(0.5 * jnp.sum(direction * image), ('grp', 'dev'))  154 us
    ppermute x10, starting transfers between devices, from_behind(): lax.ppermute(value, axis, [(i, (i + by) % length) for i in range(length)])  119 us
    dot_general x3, matrix products, per_device(): response = jnp.einsum('sij,sj->si', schur_inv, face_load, precision=highest)  29.6 us
  transfers between devices with their start and end apart: 10, of which 3 were waited for; matrix products, arithmetic and copies ran while one was open for 1% of the time, Pallas kernels for 0%

commit v1 on v0

v1 whole, which is shorter than its diff:
```python
import functools

import jax
import jax.numpy as jnp
from jax import lax
from jax.experimental import pallas as pl
from jax.experimental.pallas import tpu as pltpu
from jax.sharding import PartitionSpec as P

ITERS = 3
MESH = pl.DeviceIdType.MESH
F32 = jnp.float32
BF16 = jnp.bfloat16
N_GRP, N_DEV = 8, 32
SUB, KC, FD, FACES = 4, 24, 128, 6
ROWS = SUB * FACES
CK = SUB * KC
HI, LO = 32, 96
PIECES = 2 * CK // 8


def iota(shape, dim):
    return lax.broadcasted_iota(jnp.int32, shape, dim)


def split(x, parts):
    out = []
    for _ in range(parts - 1):
        top = x.astype(BF16)
        out.append(top)
        x = x - top.astype(F32)
    out.append(x.astype(BF16))
    return out


def dot(a, b):
    return jnp.dot(a, b, preferred_element_type=F32)


def dot_nt(a, b):
    return lax.dot_general(a, b, (((1,), (1,)), ((), ())), preferred_element_type=F32)


def pick_rows(one_hot, x):
    return sum(dot(one_hot, part) for part in split(x, 3))


def lane_sums(x):
    ones = jnp.ones((8, x.shape[1]), BF16)
    return sum(dot_nt(ones, part) for part in split(x, 3))[0:1]


def total(x):
    return jnp.sum(jnp.sum(x, axis=0, keepdims=True), axis=1, keepdims=True)


def await_bytes(ref, sem):
    pltpu.make_async_copy(ref, ref, sem).wait()


def kernel(
    gap_hbm, wgt_hbm, links_hbm, lens_hbm, schur_hbm, map_hbm, coup_hbm, coarse_hbm,
    x_out, r_out,
    gap_v, wgt_v, links_v, lens_v, map_v, schur_v, coup_v, coarse_v, coarse_p,
    fields0, sent0, fields, sent, target, sign_mask, tmp, tmp2,
    meta, tiles_a, tiles_b, coup_a, coup_x, own_w, next_w,
    high_mask, low_hot, gather_hi, gather_lo, acc_v, coarse_b,
    round1, round2, round3,
    local_sem, send_sem, recv_sem,
):
    g, d = lax.axis_index("grp"), lax.axis_index("dev")
    lane = iota((8, FD), 1)
    lane1 = iota((1, FD), 1)

    loads = [
        pltpu.make_async_copy(gap_hbm, gap_v, local_sem.at[0]),
        pltpu.make_async_copy(wgt_hbm, wgt_v, local_sem.at[1]),
        pltpu.make_async_copy(links_hbm, links_v, local_sem.at[2]),
        pltpu.make_async_copy(lens_hbm, lens_v, local_sem.at[3]),
        pltpu.make_async_copy(map_hbm, map_v, local_sem.at[4]),
    ]
    loads += [
        pltpu.make_async_copy(coup_hbm.at[s], coup_v.at[pl.ds(KC * s, KC), :], local_sem.at[5 + s])
        for s in range(SUB)
    ]
    loads.append(pltpu.make_async_copy(coarse_hbm, coarse_v, local_sem.at[9]))
    loads += [
        pltpu.make_async_copy(
            schur_hbm.at[s], schur_v.at[pl.ds(768 * s, 768), :], local_sem.at[10 + s]
        )
        for s in range(SUB)
    ]

    barrier = pltpu.get_barrier_semaphore()

    def greet(axis, n):
        def body(k, c):
            t = lax.rem(lax.axis_index(axis) + k, n)
            pl.semaphore_signal(barrier, inc=1, device_id={axis: t}, device_id_type=MESH)
            return c

        lax.fori_loop(1, n, body, 0)

    own_rows = pl.ds(pl.multiple_of(4 * d, 4), 4)
    for buf in [fields0.at[i] for i in range(2)] + [fields.at[i] for i in range(ITERS)]:
        buf[own_rows, :] = jnp.zeros((4, FD), F32)
        buf[160:256, :] = jnp.zeros((96, FD), F32)
    meta[32:128, :] = jnp.zeros((96, FD), F32)
    greet("dev", N_DEV)
    greet("grp", N_GRP)
    for load in loads:
        load.start()

    def send(src, dst, sem, axis, t):
        pltpu.make_async_remote_copy(
            src_ref=src, dst_ref=dst, send_sem=send_sem.at[sem], recv_sem=recv_sem.at[sem],
            device_id={axis: t}, device_id_type=MESH,
        ).start()

    def send_all(axis, n, src_of, dst, sem):
        def body(k, c):
            t = lax.rem(lax.axis_index(axis) + k, n)
            send(src_of(t), dst, sem, axis, t)
            return c

        lax.fori_loop(1, n, body, 0)

    acc_v[...] = jnp.zeros_like(acc_v)
    tmp[...] = jnp.zeros_like(tmp)
    tmp2[...] = jnp.zeros_like(tmp2)

    for load in loads[:5]:
        load.wait()
    links = links_v[...].astype(F32)
    tmp[0:SUB, 0:KC] = map_v[...].astype(F32)
    tmp2[0:SUB, 0:4] = links
    map_rows, link_rows = tmp[...], tmp2[...]
    meta_row = jnp.zeros((1, FD), F32)
    for s in range(SUB):
        meta_row += pltpu.roll(map_rows, KC * s, 1)[s : s + 1] if s else map_rows[0:1]
        meta_row += pltpu.roll(link_rows, CK + 4 * s, 1)[s : s + 1]
    meta[pl.ds(d, 1), :] = meta_row

    plus_dev = jnp.floor(links[0:1, 0:1] * 0.25)
    to_plus = (iota((N_DEV * SUB, FD), 0) // SUB).astype(F32) == plus_dev

    def chosen(values):
        first = jnp.concatenate([values[8:12]] * 32, axis=0)
        second = jnp.concatenate([values[12:16]] * 32, axis=0)
        return jnp.where(to_plus, first, second)

    own0 = []
    for i, src in enumerate((gap_v, wgt_v)):
        for f in range(FACES):
            fields0[i, 128 + 4 * f : 132 + 4 * f, :] = src[:, FD * f : FD * (f + 1)]
        values = fields0[i, 128:152, :]
        own0.append(values)
        sent0[i] = chosen(values)

    up, down = lax.rem(g + 1, N_GRP), lax.rem(g + N_GRP - 1, N_GRP)
    pl.semaphore_wait(barrier, N_DEV + N_GRP - 2)

    def send_fields(buf, out, sem):
        send_all(
            "dev", N_DEV,
            lambda t: out.at[pl.ds(pl.multiple_of(4 * t, 4), 4), :],
            buf.at[pl.ds(pl.multiple_of(4 * d, 4), 4), :], sem,
        )
        send(buf.at[pl.ds(132, 4), :], buf.at[pl.ds(152, 4), :], sem, "grp", down)
        send(buf.at[pl.ds(128, 4), :], buf.at[pl.ds(156, 4), :], sem, "grp", up)

    def await_fields(buf, sems, sem):
        await_bytes(buf.at[pl.ds(0, 4 * (N_DEV + 1)), :], sems.at[sem])

    S_F0, S_META, S_TA, S_TB, S_CX, S_F, S_R1, S_R2, S_R3 = 0, 2, 3, 4, 5, 6, 9, 12, 15

    for i in range(2):
        send_fields(fields0.at[i], sent0.at[i], S_F0 + i)
    own_meta = meta.at[pl.ds(d, 1), :]
    send_all("dev", N_DEV, lambda t: own_meta, own_meta, S_META)
    send(own_meta, meta.at[pl.ds(32, 1), :], S_META, "grp", down)
    send(own_meta, meta.at[pl.ds(33, 1), :], S_META, "grp", up)
    for load in loads[5:9]:
        load.wait()
    for j in range(PIECES):
        @pl.when(d != j)
        def _():
            send(
                coup_v.at[pl.ds(8 * (j % 12), 8), pl.ds(FD * (2 + j // 12), FD)],
                tiles_a.at[pl.ds(pl.multiple_of(8 * d, 8), 8), :], S_TA, "dev", j,
            )
    send(coup_v.at[:, pl.ds(FD, FD)], coup_x.at[0], S_CX, "grp", down)
    send(coup_v.at[:, pl.ds(0, FD)], coup_x.at[1], S_CX, "grp", up)

    row24 = iota((ROWS, FD), 0)
    sign = (1 - 2 * (lax.rem(row24 // 4, 2))).astype(F32)
    sign_mask[0:8, :] = sign[0:8]
    lens = lens_v[...]
    for k in range(4):
        live = iota((SUB, FD), 1) < lens[:, k : k + 1]
        sign_mask[8 + 4 * k : 12 + 4 * k, :] = jnp.where(live, 1.0 - 2.0 * (k % 2), 0.0)
    jump_sign = sign_mask[...]
    slot = iota((SUB, FD), 0).astype(F32)
    slot_of = links - 4.0 * jnp.floor(links * 0.25)
    ones4 = jnp.ones((SUB, FD), F32)
    target[0:4, :] = slot + 152.0
    target[4:8, :] = slot + 156.0
    target[8:12, :] = ones4 * links[:, 0:1]
    target[12:16, :] = ones4 * links[:, 1:2]
    target[16:20, :] = ones4 * (slot_of[:, 2:3] + 148.0)
    target[20:24, :] = ones4 * (slot_of[:, 3:4] + 144.0)
    targets = jnp.concatenate([target[...]] * 2, axis=1)
    opposite_hot = (targets == iota((ROWS, 256), 1).astype(F32)).astype(BF16)

    loads[9].wait()
    coarse_p[...] = jnp.zeros_like(coarse_p)
    for j in range(HI):
        coarse_p[:, FD * j : FD * j + LO] = coarse_v[:, LO * j : LO * (j + 1)]
    for f in range(FACES):
        for s in range(SUB):
            r = f * SUB + s
            own_w[f, KC * s : KC * (s + 1), :] = (
                coup_v[KC * s : KC * (s + 1), FD * f : FD * (f + 1)] * jump_sign[r : r + 1]
            )

    for i in range(2):
        await_fields(fields0.at[i], recv_sem, S_F0 + i)
    residual = jump_sign * (own0[0] - pick_rows(opposite_hot, fields0[0]))
    scaling = own0[1] + pick_rows(opposite_hot, fields0[1])
    scaled = scaling * residual
    result = jnp.zeros_like(residual)
    direction = image_dir = local_dir = None
    coarse_dir = norm_before = curve_before = None

    for it in range(ITERS):
        load_now = sign * scaled
        for s in range(SUB):
            part = jnp.zeros((KC, FD), F32)
            for f in range(FACES):
                r = f * SUB + s
                part += coup_v[KC * s : KC * (s + 1), FD * f : FD * (f + 1)] * load_now[r : r + 1]
            acc_v[KC * s : KC * (s + 1), :] = part
        r1, r2, r3 = round1.at[it], round2.at[it], round3.at[it]
        r1[pl.ds(d, 1), :] = lane_sums(acc_v[...])
        own = r1.at[pl.ds(d, 1), :]
        send_all("dev", N_DEV, lambda t: own, own, S_R1 + it)

        if it == 0:
            for load in loads[10:]:
                load.wait()
        response = jnp.zeros((ROWS, FD), F32)
        for s in range(SUB):
            def block(f, out):
                rows = pl.ds(pl.multiple_of(768 * s + FD * f, FD), FD)
                part = jnp.zeros((FD, FD), F32)
                for h in range(FACES):
                    r = h * SUB + s
                    part += schur_v[rows, FD * h : FD * (h + 1)] * load_now[r : r + 1]
                put = jnp.where(row24 == f * SUB + s, 1.0, 0.0).astype(BF16)
                for piece in split(part, 3):
                    out += dot_nt(put, piece)
                return out

            response = lax.fori_loop(0, FACES, block, response)
        buf, out = fields.at[it], sent.at[it]
        buf[128:152, :] = response
        out[...] = chosen(response)
        send_fields(buf, out, S_F + it)
        norm_part = 0.5 * total(residual * scaled)
        curve_part = total(load_now * response)
        cross_part = None
        if it:
            cross_part = total(load_now * local_dir + sign * direction * response)

        if it == 0:
            await_bytes(meta.at[pl.ds(0, N_DEV + 1), :], recv_sem.at[S_META])
            table = meta[...]
            high = jnp.floor((table + 0.5) * (1.0 / LO))
            low = table - LO * high
            hi_rows = iota((HI, FD), 0).astype(F32)
            lo_rows = iota((FD, FD), 0).astype(F32)
            for j in range(N_DEV):
                cols = slice(FD * j, FD * (j + 1))
                high_mask[:, cols] = jnp.where(hi_rows == high[j : j + 1], 1.0, 0.0)
                low_hot[:, cols] = jnp.where(lo_rows == low[j : j + 1], 1.0, 0.0).astype(BF16)

            @pl.when(d < PIECES)
            def _():
                tiles_a[pl.ds(pl.multiple_of(8 * d, 8), 8), :] = coup_v[
                    pl.ds(pl.multiple_of(8 * lax.rem(d, 12), 8), 8),
                    pl.ds(pl.multiple_of(FD * (2 + d // 12), FD), FD),
                ]
                await_bytes(tiles_a.at[pl.ds(0, 8 * (N_DEV - 1)), :], recv_sem.at[S_TA])
                spread = jnp.where(
                    iota((256, FD), 0) // 8 == iota((256, FD), 1), 1.0, 0.0
                ).astype(BF16)
                wanted = dot(spread, table.astype(BF16))
                which = CK + 1 - d // 12
                source = jnp.sum(
                    jnp.where(iota((256, FD), 1) == which, wanted, 0.0), axis=1, keepdims=True
                )
                source = 8.0 * jnp.floor(source * 0.25) + lax.rem(
                    iota((256, 1), 0), 8
                ).astype(F32)
                hot = jnp.where(iota((256, 256), 1).astype(F32) == source, 1.0, 0.0).astype(BF16)
                tiles_b[...] = pick_rows(hot, tiles_a[...])
                here = pl.ds(pl.multiple_of(8 * d, 8), 8)
                coup_a[here, :] = tiles_b[here, :]
                send_all(
                    "dev", N_DEV,
                    lambda t: tiles_b.at[pl.ds(pl.multiple_of(8 * t, 8), 8), :],
                    coup_a.at[here, :], S_TB,
                )

        await_bytes(r1.at[pl.ds(0, N_DEV - 1), :], recv_sem.at[S_R1 + it])
        corner = r1[...]
        top = corner.astype(BF16).astype(F32)
        rest = corner - top
        summed = jnp.zeros((2 * HI, FD), F32)
        for c in range(N_DEV // 2):
            pieces = []
            for source in (top, rest):
                pieces.append(
                    jnp.concatenate(
                        [
                            high_mask[:, FD * j : FD * (j + 1)] * source[j : j + 1]
                            for j in (2 * c, 2 * c + 1)
                        ],
                        axis=1,
                    )
                )
            both = jnp.concatenate(pieces, axis=0).astype(BF16)
            summed += dot_nt(both, low_hot[:, 256 * c : 256 * (c + 1)])
        slab_rhs = summed[0:HI] + summed[HI:]
        coarse_b[...] = slab_rhs
        part = jnp.zeros((CK, FD), F32)
        for j in range(HI):
            part += coarse_p[:, FD * j : FD * (j + 1)] * slab_rhs[j : j + 1]
        acc_v[0:CK, :] = part
        row = lane_sums(acc_v[...])
        row = jnp.where(lane1 == LO, norm_part, row)
        row = jnp.where(lane1 == LO + 1, curve_part, row)
        if it:
            row = jnp.where(lane1 == LO + 2, cross_part, row)
        r2[pl.ds(2 * g, 1), :] = row
        r2[pl.ds(2 * g + 1, 1), :] = coarse_b[pl.ds(d, 1), :]
        mine = r2.at[pl.ds(pl.multiple_of(2 * g, 2), 2), :]
        send_all("grp", N_GRP, lambda t: mine, mine, S_R2 + it)

        if it == 0:
            columns = table.T[0:CK]
            lane_f = iota((CK, FD), 1).astype(F32)

            def column(device):
                return jnp.sum(jnp.where(lane_f == device, columns, 0.0), axis=1, keepdims=True)

            def permuted(values, k):
                groups = []
                for s in range(SUB):
                    got = jnp.zeros((KC, FD), F32)
                    for j in range(SUB):
                        same = slot_of[s : s + 1, k : k + 1] == float(j)
                        got = jnp.where(same, values[KC * j : KC * (j + 1)], got)
                    groups.append(got)
                return jnp.concatenate(groups, axis=0)

            wide = jnp.zeros((CK, FD), F32)
            own_map = column(d.astype(F32)) + wide
            minus_dev = jnp.floor(links[0:1, 1:2] * 0.25)
            maps = [
                own_map,
                column(32.0) + wide,
                column(33.0) + wide,
                permuted(column(plus_dev) + wide, 0),
                permuted(column(minus_dev) + wide, 1),
                permuted(own_map, 2),
                permuted(own_map, 3),
            ]
            for i, m in enumerate(maps):
                high = jnp.floor((m + 0.5) * (1.0 / LO))
                rows = slice(CK * i, CK * (i + 1))
                gather_hi[rows, :] = jnp.where(high == lane_f, 1.0, 0.0).astype(BF16)
                gather_lo[rows, :] = jnp.where(m - LO * high == lane_f, 1.0, 0.0)

        await_bytes(r2.at[pl.ds(0, 2 * (N_GRP - 1)), :], recv_sem.at[S_R2 + it])
        pairs = r2[...]
        even = lax.rem(iota((2 * N_GRP, FD), 0), 2) == 0
        sol_row = jnp.sum(jnp.where(even, pairs, 0.0), axis=0, keepdims=True)
        rhs_row = jnp.sum(jnp.where(even, 0.0, pairs), axis=0, keepdims=True)
        row = jnp.where(
            lane1 == LO + 3, jnp.sum(sol_row * rhs_row, axis=1, keepdims=True), sol_row
        )
        if it:
            row = jnp.where(
                lane1 == LO + 4, jnp.sum(sol_row * coarse_dir, axis=1, keepdims=True), row
            )
        r3[pl.ds(d, 1), :] = row
        own3 = r3.at[pl.ds(d, 1), :]
        send_all("dev", N_DEV, lambda t: own3, own3, S_R3 + it)

        await_fields(buf, recv_sem, S_F + it)
        local_jump = jump_sign * (response - pick_rows(opposite_hot, buf[...]))
        if it == 0:
            @pl.when(d < PIECES)
            def _():
                await_bytes(coup_a.at[pl.ds(0, 8 * (PIECES - 1)), :], recv_sem.at[S_TB])

            @pl.when(d >= PIECES)
            def _():
                await_bytes(coup_a.at[pl.ds(0, 8 * PIECES), :], recv_sem.at[S_TB])

            await_bytes(coup_x, recv_sem.at[S_CX])
            beyond = [
                coup_x[0],
                coup_x[1],
                permuted(coup_a[CK : 2 * CK, :], 0),
                permuted(coup_a[0:CK, :], 1),
                permuted(coup_v[:, FD * 5 : FD * 6], 2),
                permuted(coup_v[:, FD * 4 : FD * 5], 3),
            ]
            for f in range(FACES):
                for s in range(SUB):
                    r = f * SUB + s
                    next_w[f, KC * s : KC * (s + 1), :] = (
                        -jump_sign[r : r + 1] * beyond[f][KC * s : KC * (s + 1)]
                    )

        await_bytes(r3.at[pl.ds(0, N_DEV - 1), :], recv_sem.at[S_R3 + it])
        coarse_sol = r3[...]
        sums = jnp.sum(coarse_sol, axis=0, keepdims=True)
        norm_now = sums[:, LO : LO + 1]
        curve = sums[:, LO + 1 : LO + 2] + sums[:, LO + 3 : LO + 4]
        padded = jnp.concatenate([coarse_sol, jnp.zeros((FD - HI, FD), F32)], axis=0)
        at_corner = []
        sol_parts = split(padded, 3)
        for i in range(7):
            rows = slice(CK * i, CK * (i + 1))
            hot = gather_hi[rows, :]
            got = sum(dot(hot, p) for p in sol_parts) * gather_lo[rows, :]
            at_corner.append(jnp.sum(got, axis=1, keepdims=True))
        for f in range(FACES):
            both = own_w[f] * at_corner[0] + next_w[f] * at_corner[1 + f]
            for s in range(SUB):
                r = f * SUB + s
                target[r : r + 1, :] = jnp.sum(
                    both[KC * s : KC * (s + 1)], axis=0, keepdims=True
                )
        image = local_jump + target[...]

        if it == 0:
            direction, image_dir, local_dir, coarse_dir = scaled, image, response, rhs_row
        else:
            ratio = norm_now / norm_before
            cross = sums[:, LO + 2 : LO + 3] + 2.0 * sums[:, LO + 4 : LO + 5]
            curve = curve + ratio * cross + ratio * ratio * curve_before
            direction = scaled + ratio * direction
            image_dir = image + ratio * image_dir
            local_dir = response + ratio * local_dir
            coarse_dir = rhs_row + ratio * coarse_dir
        step = norm_now / curve
        norm_before, curve_before = norm_now, curve
        result = result + step * direction
        residual = residual - step * image_dir
        scaled = scaling * residual

    for f in range(FACES):
        x_out[:, FD * f : FD * (f + 1)] = result[4 * f : 4 * f + 4]
        r_out[:, FD * f : FD * (f + 1)] = residual[4 * f : 4 * f + 4]

    for i in range(2):
        await_fields(fields0.at[i], send_sem, S_F0 + i)
    await_bytes(meta.at[pl.ds(0, N_DEV + 1), :], send_sem.at[S_META])

    @pl.when(d < PIECES)
    def _():
        await_bytes(tiles_a.at[pl.ds(0, 8 * (PIECES - 1)), :], send_sem.at[S_TA])
        await_bytes(tiles_b.at[pl.ds(0, 8 * (N_DEV - 1)), :], send_sem.at[S_TB])

    @pl.when(d >= PIECES)
    def _():
        await_bytes(tiles_a.at[pl.ds(0, 8 * PIECES), :], send_sem.at[S_TA])

    await_bytes(coup_x, send_sem.at[S_CX])
    for it in range(ITERS):
        await_fields(fields.at[it], send_sem, S_F + it)
        await_bytes(round1.at[it].at[pl.ds(0, N_DEV - 1), :], send_sem.at[S_R1 + it])
        await_bytes(round2.at[it].at[pl.ds(0, 2 * (N_GRP - 1)), :], send_sem.at[S_R2 + it])
        await_bytes(round3.at[it].at[pl.ds(0, N_DEV - 1), :], send_sem.at[S_R3 + it])


def per_device(*args):
    vmem = lambda *shape: pltpu.VMEM(shape, F32)
    field = jax.ShapeDtypeStruct((SUB, FACES * FD), F32)
    return pl.pallas_call(
        kernel,
        out_shape=(field, field),
        in_specs=[pl.BlockSpec(memory_space=pl.ANY)] * 8,
        out_specs=(pl.BlockSpec(memory_space=pltpu.VMEM),) * 2,
        scratch_shapes=[
            vmem(SUB, 768), vmem(SUB, 768),
            pltpu.VMEM((SUB, 4), jnp.int32), pltpu.VMEM((SUB, 4), jnp.int32),
            pltpu.VMEM((SUB, KC), jnp.int32),
            vmem(SUB * 768, 768), vmem(CK, 768), vmem(CK, 3072), vmem(CK, HI * FD),
            vmem(2, 256, FD), vmem(2, 128, FD),
            vmem(ITERS, 256, FD), vmem(ITERS, 128, FD),
            vmem(ROWS, FD), vmem(ROWS, FD), vmem(8, FD), vmem(8, FD),
            vmem(FD, FD), vmem(256, FD), vmem(256, FD), vmem(2 * CK, FD), vmem(2, CK, FD),
            vmem(FACES, CK, FD), vmem(FACES, CK, FD),
            vmem(HI, HI * FD), pltpu.VMEM((FD, HI * FD), BF16),
            pltpu.VMEM((7 * CK, FD), BF16), vmem(7 * CK, FD), vmem(FD, FD), vmem(HI, FD),
            vmem(ITERS, N_DEV, FD), vmem(ITERS, 2 * N_GRP, FD), vmem(ITERS, N_DEV, FD),
            pltpu.SemaphoreType.DMA((14,)),
            pltpu.SemaphoreType.DMA((18,)),
            pltpu.SemaphoreType.DMA((18,)),
        ],
        compiler_params=pltpu.CompilerParams(
            collective_id=0, has_side_effects=True, vmem_limit_bytes=48 * 1024 * 1024
        ),
    )(*args)


def solution(mesh):
    return jax.shard_map(
        per_device,
        mesh=mesh,
        in_specs=(
            P(("grp", "dev"), None),
            P(("grp", "dev"), None),
            P("dev", None),
            P("dev", None),
            P(("grp", "dev"), None, None),
            P(("grp", "dev"), None),
            P(("grp", "dev"), None, None),
            P("dev", None),
        ),
        out_specs=(P(("grp", "dev"), None), P(("grp", "dev"), None)),
        check_vma=False,
    )
```

time: 1310 us -> 79.6 us (0.06)
  blocking collectives: 1120 us -> 0 us
  starting transfers between devices: 119 us -> 0 us
  Pallas kernels: 0 us -> 71.7 us
  matrix products: 42.6 us -> 0 us
    psum x8 -> x0, blocking collectives: 620 us -> none  [the longest x3 243 us: per_device(): coarse_rhs = lax.psum(operator_local_rhs, ('grp', 'dev'))]
    unnamed x3 -> x0, blocking collectives: 337 us -> none
    all_gather x5 -> x0, blocking collectives: 159 us -> none  [opposite(): lax.all_gather(values[:, 2:4].reshape(subdomains, 2 * face_width), 'dev',...]
    ppermute x10 -> x0, starting transfers between devices: 119 us -> none  [from_behind(): lax.ppermute(value, axis, [(i, (i + by) % length) for i in range(length)])]
    pallas_call x0 -> x1, Pallas kernels: none -> 71.7 us  [per_device(): pl.pallas_call(kernel, out_shape=(field, field), in_specs=[pl.BlockSpec(m...]
    dot_general x38 -> x0, matrix products: 42.6 us -> none  [the longest x3 29.6 us: per_device(): response = jnp.einsum('sij,sj->si', schur_inv, face_load, precision=highest)]
  transfers between devices with their start and end apart: 10 -> 0, of which waited for: 3 -> 0; matrix products, arithmetic and copies ran while one was open for 1% -> 0% of each run, Pallas kernels for 0% -> 0%
where the time goes in v1:
time: 79.6 us; the launch traced here: 79.2 us
  Pallas kernels  71.7 us (90%)
  local copies, waits for them, and re-layouts  6.88 us (9%)
    pallas_call x1, Pallas kernels, per_device(): pl.pallas_call(kernel, out_shape=(field, field), in_specs=[pl.BlockSpec(m...  71.7 us
    unnamed x16, local copies, waits for them, and re-layouts  6.88 us

profile of v1, /device:TPU:1, one launch (start us, length us, event | category | flops | bytes accessed | tf_op | source)
XLA Modules:
  0.0 79.2 jit_solution(7577301744815483271)
XLA Ops:
  0.6 0.0 copy-start
  0.6 1.3 %copy-done = f32[96,3072]{1,0:T(8,128)S(1)} copy-done((f32[96,3072]{1,0:T(8,128)S(1)}, f32[96,3072]{1,0:T(8,128)}, u32[]{:S(2)}) %copy-start) | copy-done | bytes 1179672
  1.9 0.0 copy-start.1
  1.9 1.0 %copy-done.1 = f32[4,24,768]{2,1,0:T(8,128)S(1)} copy-done((f32[4,24,768]{2,1,0:T(8,128)S(1)}, f32[4,24,768]{2,1,0:T(8,128)}, u32[]{:S(2)}) %copy-start.1) | copy-done | bytes 294936
  2.9 0.0 copy-start.2
  2.9 0.7 copy-done.2
  3.6 0.0 copy-start.3
  3.6 0.7 copy-done.3
  4.3 0.0 copy-start.4
  4.3 0.7 copy-done.4
  5.0 0.0 copy-start.5
  5.0 0.7 copy-done.5
  5.6 0.0 copy-start.6
  5.6 0.7 copy-done.6
  6.3 71.7 %shard_map.95 = (f32[4,768]{1,0:T(4,128)S(1)}, f32[4,768]{1,0:T(4,128)S(1)}) custom-call(f32[4,768]{1,0:T(4,128)S(1)} %copy-done.2, f32[4,768]{1,0:T(4,128)S(1)} %copy-done.3, s32[4,4]{1,0:T(4,128)S(1)} %copy-done.4, s32[4,4]{1,0:T(4,128)S(1)} %copy-done.5, f32[4,768,768]{2,1,0:T(8,128)} %schur_hbm.1, s32[4,24]{1,0:T(4,128)S(1)} %copy-done.6, ...), custom_call_target="tpu_custom_call" | custom-call | tf_op jit(solution)/shard_map/pallas_call | solution.py:494
  78.0 0.6 copy.12
  78.6 0.6 copy.13
Async XLA Ops:
  0.6 1.3 %copy-start = (f32[96,3072]{1,0:T(8,128)S(1)}, f32[96,3072]{1,0:T(8,128)}, u32[]{:S(2)}) copy-start(f32[96,3072]{1,0:T(8,128)} %coarse_hbm.1) | copy-start | bytes 3538948
  1.9 1.0 %copy-start.1 = (f32[4,24,768]{2,1,0:T(8,128)S(1)}, f32[4,24,768]{2,1,0:T(8,128)}, u32[]{:S(2)}) copy-start(f32[4,24,768]{2,1,0:T(8,128)} %coup_hbm.1) | copy-start | bytes 884740
  2.9 0.7 copy-start.2
  3.6 0.7 copy-start.3
  4.3 0.7 copy-start.4
  5.0 0.7 copy-start.5
  5.6 0.7 copy-start.6

commit v2 on v1

--- a/solution.py
+++ b/solution.py
@@ -64,7 +64,7 @@
     gap_v, wgt_v, links_v, lens_v, map_v, schur_v, coup_v, coarse_v, coarse_p,
     fields0, sent0, fields, sent, target, sign_mask, tmp, tmp2,
     meta, tiles_a, tiles_b, coup_a, coup_x, own_w, next_w,
-    high_mask, low_hot, gather_hi, gather_lo, acc_v, coarse_b,
+    high_mask, low_hot, gather_hi, gather_lo, acc_v, coarse_b, products,
     round1, round2, round3,
     local_sem, send_sem, recv_sem,
 ):
@@ -193,6 +193,9 @@
     send(coup_v.at[:, pl.ds(0, FD)], coup_x.at[1], S_CX, "grp", up)
 
     row24 = iota((ROWS, FD), 0)
+    row_of_lane = jnp.where(
+        iota((ROWS, ROWS * FD), 1) // FD == iota((ROWS, ROWS * FD), 0), 1.0, 0.0
+    ).astype(BF16)
     sign = (1 - 2 * (lax.rem(row24 // 4, 2))).astype(F32)
     sign_mask[0:8, :] = sign[0:8]
     lens = lens_v[...]
@@ -248,20 +251,19 @@
         if it == 0:
             for load in loads[10:]:
                 load.wait()
-        response = jnp.zeros((ROWS, FD), F32)
         for s in range(SUB):
-            def block(f, out):
+            rows_of_load = [load_now[h * SUB + s : h * SUB + s + 1] for h in range(FACES)]
+
+            def block(f, c):
                 rows = pl.ds(pl.multiple_of(768 * s + FD * f, FD), FD)
-                part = jnp.zeros((FD, FD), F32)
-                for h in range(FACES):
-                    r = h * SUB + s
-                    part += schur_v[rows, FD * h : FD * (h + 1)] * load_now[r : r + 1]
-                put = jnp.where(row24 == f * SUB + s, 1.0, 0.0).astype(BF16)
-                for piece in split(part, 3):
-                    out += dot_nt(put, piece)
-                return out
-
-            response = lax.fori_loop(0, FACES, block, response)
+                part = schur_v[rows, 0:FD] * rows_of_load[0]
+                for h in range(1, FACES):
+                    part += schur_v[rows, FD * h : FD * (h + 1)] * rows_of_load[h]
+                products[:, pl.ds(pl.multiple_of(FD * (f * SUB + s), FD), FD)] = part
+                return c
+
+            lax.fori_loop(0, FACES, block, 0)
+        response = sum(dot_nt(row_of_lane, part) for part in split(products[...], 2))
         buf, out = fields.at[it], sent.at[it]
         buf[128:152, :] = response
         out[...] = chosen(response)
@@ -494,7 +496,7 @@
     return pl.pallas_call(
         kernel,
         out_shape=(field, field),
-        in_specs=[pl.BlockSpec(memory_space=pl.ANY)] * 8,
+        in_specs=[pl.BlockSpec(memory_space=pltpu.HBM)] * 8,
         out_specs=(pl.BlockSpec(memory_space=pltpu.VMEM),) * 2,
         scratch_shapes=[
             vmem(SUB, 768), vmem(SUB, 768),
@@ -507,14 +509,14 @@
             vmem(FD, FD), vmem(256, FD), vmem(256, FD), vmem(2 * CK, FD), vmem(2, CK, FD),
             vmem(FACES, CK, FD), vmem(FACES, CK, FD),
             vmem(HI, HI * FD), pltpu.VMEM((FD, HI * FD), BF16),
-            pltpu.VMEM((7 * CK, FD), BF16), vmem(7 * CK, FD), vmem(FD, FD), vmem(HI, FD),
+            pltpu.VMEM((7 * CK, FD), BF16), vmem(7 * CK, FD), vmem(FD, FD), vmem(HI, FD), vmem(FD, ROWS * FD),
             vmem(ITERS, N_DEV, FD), vmem(ITERS, 2 * N_GRP, FD), vmem(ITERS, N_DEV, FD),
             pltpu.SemaphoreType.DMA((14,)),
             pltpu.SemaphoreType.DMA((18,)),
             pltpu.SemaphoreType.DMA((18,)),
         ],
         compiler_params=pltpu.CompilerParams(
-            collective_id=0, has_side_effects=True, vmem_limit_bytes=48 * 1024 * 1024
+            collective_id=0, has_side_effects=True, vmem_limit_bytes=63 * 1024 * 1024
         ),
     )(*args)
 

time: 79.6 us -> 74.2 us (0.932)
  local copies, waits for them, and re-layouts: 6.88 us -> 2.61 us
  Pallas kernels: 71.7 us -> 70.6 us
    unnamed x16 -> x2, local copies, waits for them, and re-layouts: 6.88 us -> 2.61 us
    pallas_call x1, Pallas kernels: 71.7 us -> 70.6 us  [per_device(): pl.pallas_call(kernel, out_shape=(field, field), in_specs=[pl.BlockSpec(m...]
where the time goes in v2:
time: 74.2 us; the launch traced here: 73.8 us
  Pallas kernels  70.6 us (95%)
  local copies, waits for them, and re-layouts  2.61 us (4%)
    pallas_call x1, Pallas kernels, per_device(): pl.pallas_call(kernel, out_shape=(field, field), in_specs=[pl.BlockSpec(m...  70.6 us
    unnamed x2, local copies, waits for them, and re-layouts  2.61 us

profile of v2, /device:TPU:1, one launch (start us, length us, event | category | flops | bytes accessed | tf_op | source)
XLA Modules:
  0.0 73.8 jit_solution(3471323032856191376)
XLA Ops:
  0.6 70.6 %shard_map.95 = (f32[4,768]{1,0:T(4,128)}, f32[4,768]{1,0:T(4,128)}) custom-call(f32[4,768]{1,0:T(4,128)} %gap_hbm.1, f32[4,768]{1,0:T(4,128)} %wgt_hbm.1, s32[4,4]{1,0:T(4,128)} %links_hbm.1, s32[4,4]{1,0:T(4,128)} %lens_hbm.1, f32[4,768,768]{2,1,0:T(8,128)} %schur_hbm.1, s32[4,24]{1,0:T(4,128)} %map_hbm.1, f32[4,24,768]{2,1,0:T(8,128)} %coup_hbm.1, ...), custom_call_target="tpu_custom_call" | custom-call | tf_op jit(solution)/shard_map/pallas_call | solution.py:496
  71.2 1.3 %copy.12 = f32[4,768]{1,0:T(4,128)} copy(f32[4,768]{1,0:T(4,128)} %get-tuple-element.4) | data formatting | bytes 24576
  72.5 1.3 %copy.13 = f32[4,768]{1,0:T(4,128)} copy(f32[4,768]{1,0:T(4,128)} %get-tuple-element.5) | data formatting | bytes 24576

commit v3 on v2

--- a/solution.py
+++ b/solution.py
@@ -16,6 +16,7 @@
 ROWS = SUB * FACES
 CK = SUB * KC
 HI, LO = 32, 96
+FAR = 8
 PIECES = 2 * CK // 8
 
 
@@ -42,12 +43,12 @@
 
 
 def pick_rows(one_hot, x):
-    return sum(dot(one_hot, part) for part in split(x, 3))
+    return sum(dot(one_hot, part) for part in split(x, 2))
 
 
 def lane_sums(x):
     ones = jnp.ones((8, x.shape[1]), BF16)
-    return sum(dot_nt(ones, part) for part in split(x, 3))[0:1]
+    return sum(dot_nt(ones, part) for part in split(x, 2))[0:1]
 
 
 def total(x):
@@ -58,13 +59,17 @@
     pltpu.make_async_copy(ref, ref, sem).wait()
 
 
+def far_first(i, n):
+    return n // 2 + (1 - 2 * lax.rem(i, 2)) * ((i + 1) // 2)
+
+
 def kernel(
     gap_hbm, wgt_hbm, links_hbm, lens_hbm, schur_hbm, map_hbm, coup_hbm, coarse_hbm,
-    x_out, r_out,
+    out_ref,
     gap_v, wgt_v, links_v, lens_v, map_v, schur_v, coup_v, coarse_v, coarse_p,
     fields0, sent0, fields, sent, target, sign_mask, tmp, tmp2,
-    meta, tiles_a, tiles_b, coup_a, coup_x, own_w, next_w,
-    high_mask, low_hot, gather_hi, gather_lo, acc_v, coarse_b, products,
+    meta, slots, tiles_a, tiles_b, coup_a, coup_x, own_w, next_w,
+    high_mask, low_hot, gather_hi, gather_lo, acc_v, coarse_b, products, placed,
     round1, round2, round3,
     local_sem, send_sem, recv_sem,
 ):
@@ -93,19 +98,38 @@
 
     barrier = pltpu.get_barrier_semaphore()
 
+    def offsets(i):
+        return far_first(i // 4, 8), far_first(lax.rem(i, 4), 4)
+
+    def slab_target(i):
+        dz, dy = offsets(i)
+        return lax.rem(d // 4 + dz, 8) * 4 + lax.rem(lax.rem(d, 4) + dy, 4)
+
+    def slab_source(i):
+        dz, dy = offsets(i)
+        return lax.rem(d // 4 + 8 - dz, 8) * 4 + lax.rem(lax.rem(d, 4) + 4 - dy, 4)
+
+    def each(axis, first, last, act):
+        def body(i, c):
+            if axis == "dev":
+                act(slab_target(i), i)
+            else:
+                act(lax.rem(g + far_first(i, N_GRP), N_GRP), i)
+            return c
+
+        lax.fori_loop(first, last, body, 0)
+
     def greet(axis, n):
-        def body(k, c):
-            t = lax.rem(lax.axis_index(axis) + k, n)
+        def act(t, i):
             pl.semaphore_signal(barrier, inc=1, device_id={axis: t}, device_id_type=MESH)
-            return c
-
-        lax.fori_loop(1, n, body, 0)
+
+        each(axis, 0, n - 1, act)
 
     own_rows = pl.ds(pl.multiple_of(4 * d, 4), 4)
     for buf in [fields0.at[i] for i in range(2)] + [fields.at[i] for i in range(ITERS)]:
         buf[own_rows, :] = jnp.zeros((4, FD), F32)
-        buf[160:256, :] = jnp.zeros((96, FD), F32)
     meta[32:128, :] = jnp.zeros((96, FD), F32)
+    slots[32:128, :] = jnp.zeros((96, FD), F32)
     greet("dev", N_DEV)
     greet("grp", N_GRP)
     for load in loads:
@@ -118,12 +142,7 @@
         ).start()
 
     def send_all(axis, n, src_of, dst, sem):
-        def body(k, c):
-            t = lax.rem(lax.axis_index(axis) + k, n)
-            send(src_of(t), dst, sem, axis, t)
-            return c
-
-        lax.fori_loop(1, n, body, 0)
+        each(axis, 0, n - 1, lambda t, i: send(src_of(t), dst, sem, axis, t))
 
     acc_v[...] = jnp.zeros_like(acc_v)
     tmp[...] = jnp.zeros_like(tmp)
@@ -172,7 +191,9 @@
     def await_fields(buf, sems, sem):
         await_bytes(buf.at[pl.ds(0, 4 * (N_DEV + 1)), :], sems.at[sem])
 
-    S_F0, S_META, S_TA, S_TB, S_CX, S_F, S_R1, S_R2, S_R3 = 0, 2, 3, 4, 5, 6, 9, 12, 15
+    S_F0, S_META, S_TA, S_TB, S_CX, S_F, S_R1, S_R2, S_R3, S_NEAR = (
+        0, 2, 3, 4, 5, 6, 9, 12, 15, 18
+    )
 
     for i in range(2):
         send_fields(fields0.at[i], sent0.at[i], S_F0 + i)
@@ -212,8 +233,8 @@
     target[12:16, :] = ones4 * links[:, 1:2]
     target[16:20, :] = ones4 * (slot_of[:, 2:3] + 148.0)
     target[20:24, :] = ones4 * (slot_of[:, 3:4] + 144.0)
-    targets = jnp.concatenate([target[...]] * 2, axis=1)
-    opposite_hot = (targets == iota((ROWS, 256), 1).astype(F32)).astype(BF16)
+    targets = target[...][:, 0:1]
+    opposite_hot = jnp.where(targets == iota((ROWS, 160), 1).astype(F32), 1.0, 0.0).astype(BF16)
 
     loads[9].wait()
     coarse_p[...] = jnp.zeros_like(coarse_p)
@@ -235,6 +256,43 @@
     direction = image_dir = local_dir = None
     coarse_dir = norm_before = curve_before = None
 
+    def scattered(loads_of, first, last):
+        parts = [part.astype(F32) for part in split(loads_of[first:last, :], 2)]
+        for j in range(first, last):
+            for q in range(2):
+                placed[HI * q : HI * (q + 1), FD * j : FD * (j + 1)] = (
+                    high_mask[:, FD * j : FD * (j + 1)] * parts[q][j - first : j - first + 1]
+                ).astype(BF16)
+        return dot(placed[:, FD * first : FD * last], low_hot[FD * first : FD * last, :])
+
+    def sends_done(it):
+        if it < 0:
+            for i in range(2):
+                await_fields(fields0.at[i], send_sem, S_F0 + i)
+            await_bytes(meta.at[pl.ds(0, N_DEV + 1), :], send_sem.at[S_META])
+
+            @pl.when(d < PIECES)
+            def _():
+                await_bytes(tiles_a.at[pl.ds(0, 8 * (PIECES - 1)), :], send_sem.at[S_TA])
+
+            @pl.when(d >= PIECES)
+            def _():
+                await_bytes(tiles_a.at[pl.ds(0, 8 * PIECES), :], send_sem.at[S_TA])
+
+            await_bytes(coup_x, send_sem.at[S_CX])
+            return
+        if it == 0:
+            @pl.when(d < PIECES)
+            def _():
+                await_bytes(tiles_b.at[pl.ds(0, 8 * (N_DEV - 1)), :], send_sem.at[S_TB])
+
+        await_fields(fields.at[it], send_sem, S_F + it)
+        one = round1.at[it]
+        await_bytes(one.at[pl.ds(0, FAR), :], send_sem.at[S_R1 + it])
+        await_bytes(one.at[pl.ds(0, N_DEV - 1 - FAR), :], send_sem.at[S_NEAR + it])
+        await_bytes(round2.at[it].at[pl.ds(0, 2 * (N_GRP - 1)), :], send_sem.at[S_R2 + it])
+        await_bytes(round3.at[it].at[pl.ds(0, N_DEV - 1), :], send_sem.at[S_R3 + it])
+
     for it in range(ITERS):
         load_now = sign * scaled
         for s in range(SUB):
@@ -244,9 +302,13 @@
                 part += coup_v[KC * s : KC * (s + 1), FD * f : FD * (f + 1)] * load_now[r : r + 1]
             acc_v[KC * s : KC * (s + 1), :] = part
         r1, r2, r3 = round1.at[it], round2.at[it], round3.at[it]
-        r1[pl.ds(d, 1), :] = lane_sums(acc_v[...])
-        own = r1.at[pl.ds(d, 1), :]
-        send_all("dev", N_DEV, lambda t: own, own, S_R1 + it)
+        r1[N_DEV - 1 :, :] = lane_sums(acc_v[...])
+        own = r1.at[pl.ds(N_DEV - 1, 1), :]
+        each("dev", 0, FAR, lambda t, i: send(own, r1.at[pl.ds(i, 1), :], S_R1 + it, "dev", t))
+        each(
+            "dev", FAR, N_DEV - 1,
+            lambda t, i: send(own, r1.at[pl.ds(i, 1), :], S_NEAR + it, "dev", t),
+        )
 
         if it == 0:
             for load in loads[10:]:
@@ -277,14 +339,21 @@
         if it == 0:
             await_bytes(meta.at[pl.ds(0, N_DEV + 1), :], recv_sem.at[S_META])
             table = meta[...]
-            high = jnp.floor((table + 0.5) * (1.0 / LO))
-            low = table - LO * high
+
+            def reorder(i, c):
+                slots[pl.ds(i, 1), :] = meta[pl.ds(slab_source(i), 1), :]
+                return c
+
+            lax.fori_loop(0, N_DEV, reorder, 0)
+            ordered = slots[...]
+            high = jnp.floor((ordered + 0.5) * (1.0 / LO))
+            low = (ordered - LO * high).T
             hi_rows = iota((HI, FD), 0).astype(F32)
-            lo_rows = iota((FD, FD), 0).astype(F32)
+            lo_lanes = iota((FD, FD), 1).astype(F32)
             for j in range(N_DEV):
                 cols = slice(FD * j, FD * (j + 1))
                 high_mask[:, cols] = jnp.where(hi_rows == high[j : j + 1], 1.0, 0.0)
-                low_hot[:, cols] = jnp.where(lo_rows == low[j : j + 1], 1.0, 0.0).astype(BF16)
+                low_hot[cols, :] = jnp.where(lo_lanes == low[:, j : j + 1], 1.0, 0.0).astype(BF16)
 
             @pl.when(d < PIECES)
             def _():
@@ -314,25 +383,12 @@
                     coup_a.at[here, :], S_TB,
                 )
 
-        await_bytes(r1.at[pl.ds(0, N_DEV - 1), :], recv_sem.at[S_R1 + it])
-        corner = r1[...]
-        top = corner.astype(BF16).astype(F32)
-        rest = corner - top
-        summed = jnp.zeros((2 * HI, FD), F32)
-        for c in range(N_DEV // 2):
-            pieces = []
-            for source in (top, rest):
-                pieces.append(
-                    jnp.concatenate(
-                        [
-                            high_mask[:, FD * j : FD * (j + 1)] * source[j : j + 1]
-                            for j in (2 * c, 2 * c + 1)
-                        ],
-                        axis=1,
-                    )
-                )
-            both = jnp.concatenate(pieces, axis=0).astype(BF16)
-            summed += dot_nt(both, low_hot[:, 256 * c : 256 * (c + 1)])
+        sends_done(it - 1)
+
+        await_bytes(r1.at[pl.ds(FAR, N_DEV - 1 - FAR), :], recv_sem.at[S_NEAR + it])
+        summed = scattered(r1, FAR, N_DEV)
+        await_bytes(r1.at[pl.ds(0, FAR), :], recv_sem.at[S_R1 + it])
+        summed += scattered(r1, 0, FAR)
         slab_rhs = summed[0:HI] + summed[HI:]
         coarse_b[...] = slab_rhs
         part = jnp.zeros((CK, FD), F32)
@@ -434,7 +490,7 @@
         curve = sums[:, LO + 1 : LO + 2] + sums[:, LO + 3 : LO + 4]
         padded = jnp.concatenate([coarse_sol, jnp.zeros((FD - HI, FD), F32)], axis=0)
         at_corner = []
-        sol_parts = split(padded, 3)
+        sol_parts = split(padded, 2)
         for i in range(7):
             rows = slice(CK * i, CK * (i + 1))
             hot = gather_hi[rows, :]
@@ -466,59 +522,42 @@
         scaled = scaling * residual
 
     for f in range(FACES):
-        x_out[:, FD * f : FD * (f + 1)] = result[4 * f : 4 * f + 4]
-        r_out[:, FD * f : FD * (f + 1)] = residual[4 * f : 4 * f + 4]
-
-    for i in range(2):
-        await_fields(fields0.at[i], send_sem, S_F0 + i)
-    await_bytes(meta.at[pl.ds(0, N_DEV + 1), :], send_sem.at[S_META])
-
-    @pl.when(d < PIECES)
-    def _():
-        await_bytes(tiles_a.at[pl.ds(0, 8 * (PIECES - 1)), :], send_sem.at[S_TA])
-        await_bytes(tiles_b.at[pl.ds(0, 8 * (N_DEV - 1)), :], send_sem.at[S_TB])
-
-    @pl.when(d >= PIECES)
-    def _():
-        await_bytes(tiles_a.at[pl.ds(0, 8 * PIECES), :], send_sem.at[S_TA])
-
-    await_bytes(coup_x, send_sem.at[S_CX])
-    for it in range(ITERS):
-        await_fields(fields.at[it], send_sem, S_F + it)
-        await_bytes(round1.at[it].at[pl.ds(0, N_DEV - 1), :], send_sem.at[S_R1 + it])
-        await_bytes(round2.at[it].at[pl.ds(0, 2 * (N_GRP - 1)), :], send_sem.at[S_R2 + it])
-        await_bytes(round3.at[it].at[pl.ds(0, N_DEV - 1), :], send_sem.at[S_R3 + it])
+        out_ref[0, :, FD * f : FD * (f + 1)] = result[4 * f : 4 * f + 4]
+        out_ref[1, :, FD * f : FD * (f + 1)] = residual[4 * f : 4 * f + 4]
+
+    sends_done(ITERS - 1)
 
 
 def per_device(*args):
     vmem = lambda *shape: pltpu.VMEM(shape, F32)
-    field = jax.ShapeDtypeStruct((SUB, FACES * FD), F32)
-    return pl.pallas_call(
+    field = jax.ShapeDtypeStruct((2, SUB, FACES * FD), F32)
+    both = pl.pallas_call(
         kernel,
-        out_shape=(field, field),
+        out_shape=field,
         in_specs=[pl.BlockSpec(memory_space=pltpu.HBM)] * 8,
-        out_specs=(pl.BlockSpec(memory_space=pltpu.VMEM),) * 2,
+        out_specs=pl.BlockSpec(memory_space=pltpu.VMEM),
         scratch_shapes=[
             vmem(SUB, 768), vmem(SUB, 768),
             pltpu.VMEM((SUB, 4), jnp.int32), pltpu.VMEM((SUB, 4), jnp.int32),
             pltpu.VMEM((SUB, KC), jnp.int32),
             vmem(SUB * 768, 768), vmem(CK, 768), vmem(CK, 3072), vmem(CK, HI * FD),
-            vmem(2, 256, FD), vmem(2, 128, FD),
-            vmem(ITERS, 256, FD), vmem(ITERS, 128, FD),
+            vmem(2, 160, FD), vmem(2, 128, FD),
+            vmem(ITERS, 160, FD), vmem(ITERS, 128, FD),
             vmem(ROWS, FD), vmem(ROWS, FD), vmem(8, FD), vmem(8, FD),
-            vmem(FD, FD), vmem(256, FD), vmem(256, FD), vmem(2 * CK, FD), vmem(2, CK, FD),
+            vmem(FD, FD), vmem(FD, FD), vmem(256, FD), vmem(256, FD), vmem(2 * CK, FD), vmem(2, CK, FD),
             vmem(FACES, CK, FD), vmem(FACES, CK, FD),
-            vmem(HI, HI * FD), pltpu.VMEM((FD, HI * FD), BF16),
-            pltpu.VMEM((7 * CK, FD), BF16), vmem(7 * CK, FD), vmem(FD, FD), vmem(HI, FD), vmem(FD, ROWS * FD),
+            vmem(HI, HI * FD), pltpu.VMEM((HI * FD, FD), BF16),
+            pltpu.VMEM((7 * CK, FD), BF16), vmem(7 * CK, FD), vmem(FD, FD), vmem(HI, FD), vmem(FD, ROWS * FD), pltpu.VMEM((2 * HI, HI * FD), BF16),
             vmem(ITERS, N_DEV, FD), vmem(ITERS, 2 * N_GRP, FD), vmem(ITERS, N_DEV, FD),
             pltpu.SemaphoreType.DMA((14,)),
-            pltpu.SemaphoreType.DMA((18,)),
-            pltpu.SemaphoreType.DMA((18,)),
+            pltpu.SemaphoreType.DMA((21,)),
+            pltpu.SemaphoreType.DMA((21,)),
         ],
         compiler_params=pltpu.CompilerParams(
             collective_id=0, has_side_effects=True, vmem_limit_bytes=63 * 1024 * 1024
         ),
     )(*args)
+    return both[0], both[1]
 
 
 def solution(mesh):

time: 74.2 us -> 71 us (0.957)
  Pallas kernels: 70.6 us -> 68.8 us
  local copies, waits for them, and re-layouts: 2.61 us -> 1.33 us
    unnamed x2 -> x0, local copies, waits for them, and re-layouts: 2.61 us -> none
    pallas_call x1, Pallas kernels: 70.6 us -> 68.8 us  [per_device(): pl.pallas_call(kernel, out_shape=field, in_specs=[pl.BlockSpec(memory_spa...]
    squeeze x0 -> x1, local copies, waits for them, and re-layouts: none -> 1.33 us  [per_device(): return (both[0], both[1])]
where the time goes in v3:
time: 71 us; the launch traced here: 70.8 us
  Pallas kernels  68.8 us (97%)
  local copies, waits for them, and re-layouts  1.33 us (2%)
    pallas_call x1, Pallas kernels, per_device(): pl.pallas_call(kernel, out_shape=field, in_specs=[pl.BlockSpec(memory_spa...  68.8 us

profile of v3, /device:TPU:1, one launch (start us, length us, event | category | flops | bytes accessed | tf_op | source)
XLA Modules:
  0.0 70.8 jit_solution(12877799503644679387)
XLA Ops:
  0.6 68.8 %shard_map.95 = f32[2,4,768]{2,1,0:T(4,128)} custom-call(f32[4,768]{1,0:T(4,128)} %gap_hbm.1, f32[4,768]{1,0:T(4,128)} %wgt_hbm.1, s32[4,4]{1,0:T(4,128)} %links_hbm.1, s32[4,4]{1,0:T(4,128)} %lens_hbm.1, f32[4,768,768]{2,1,0:T(8,128)} %schur_hbm.1, s32[4,24]{1,0:T(4,128)} %map_hbm.1, f32[4,24,768]{2,1,0:T(8,128)} %coup_hbm.1, f32[96,3072]{1,0:T(8,128)} %coarse_hbm.1), custom_call_target="tpu_custom_call" | custom-call | tf_op jit(solution)/shard_map/pallas_call | solution.py:534
  69.4 1.3 %slice_bitcast_fusion = (f32[4,768]{1,0:T(4,128)}, f32[4,768]{1,0:T(4,128)}) fusion(f32[2,4,768]{2,1,0:T(4,128)} %shard_map.95), kind=kLoop, calls=%fused_computation | loop fusion | bytes 49152 | tf_op jit(solution)/shard_map/squeeze | solution.py:560

commit v4 on v3

--- a/solution.py
+++ b/solution.py
@@ -69,12 +69,12 @@
     gap_v, wgt_v, links_v, lens_v, map_v, schur_v, coup_v, coarse_v, coarse_p,
     fields0, sent0, fields, sent, target, sign_mask, tmp, tmp2,
     meta, slots, tiles_a, tiles_b, coup_a, coup_x, own_w, next_w,
-    high_mask, low_hot, gather_hi, gather_lo, acc_v, coarse_b, products, placed,
+    high_mask, low_hot, gather_hi, gather_lo, acc_v, products, placed,
     round1, round2, round3,
     local_sem, send_sem, recv_sem,
 ):
     g, d = lax.axis_index("grp"), lax.axis_index("dev")
-    lane = iota((8, FD), 1)
+    me = g * N_DEV + d
     lane1 = iota((1, FD), 1)
 
     loads = [
@@ -143,6 +143,28 @@
 
     def send_all(axis, n, src_of, dst, sem):
         each(axis, 0, n - 1, lambda t, i: send(src_of(t), dst, sem, axis, t))
+
+    def send_everywhere(src, sem):
+        near = sorted(
+            ((y, x, c) for y in range(4) for x in range(4) for c in range(2)),
+            key=lambda o: -(min(o[0], 4 - o[0]) + min(o[1], 4 - o[1])),
+        )
+
+        def to_layer(z, places):
+            for y, x, c in places:
+                to_g = lax.rem(g // 2 + x, 4) * 2 + lax.rem(g + c, 2)
+                to_d = z * 4 + lax.rem(lax.rem(d, 4) + y, 4)
+                pltpu.make_async_remote_copy(
+                    src_ref=src, dst_ref=src, send_sem=send_sem.at[sem], recv_sem=recv_sem.at[sem],
+                    device_id=(to_g, to_d), device_id_type=MESH,
+                ).start()
+
+        def layer(i, c):
+            to_layer(lax.rem(d // 4 + far_first(i, 8), 8), near)
+            return c
+
+        lax.fori_loop(0, 7, layer, 0)
+        to_layer(d // 4, [o for o in near if o != (0, 0, 0)])
 
     acc_v[...] = jnp.zeros_like(acc_v)
     tmp[...] = jnp.zeros_like(tmp)
@@ -290,8 +312,8 @@
         one = round1.at[it]
         await_bytes(one.at[pl.ds(0, FAR), :], send_sem.at[S_R1 + it])
         await_bytes(one.at[pl.ds(0, N_DEV - 1 - FAR), :], send_sem.at[S_NEAR + it])
-        await_bytes(round2.at[it].at[pl.ds(0, 2 * (N_GRP - 1)), :], send_sem.at[S_R2 + it])
-        await_bytes(round3.at[it].at[pl.ds(0, N_DEV - 1), :], send_sem.at[S_R3 + it])
+        await_bytes(round2.at[it].at[pl.ds(0, N_DEV * N_GRP - 1), :], send_sem.at[S_R2 + it])
+        await_bytes(round3.at[it].at[pl.ds(0, HI * (N_GRP - 1)), :], send_sem.at[S_R3 + it])
 
     for it in range(ITERS):
         load_now = sign * scaled
@@ -301,7 +323,7 @@
                 r = f * SUB + s
                 part += coup_v[KC * s : KC * (s + 1), FD * f : FD * (f + 1)] * load_now[r : r + 1]
             acc_v[KC * s : KC * (s + 1), :] = part
-        r1, r2, r3 = round1.at[it], round2.at[it], round3.at[it]
+        r1, rows_of_all, rhs_of_all = round1.at[it], round2.at[it], round3.at[it]
         r1[N_DEV - 1 :, :] = lane_sums(acc_v[...])
         own = r1.at[pl.ds(N_DEV - 1, 1), :]
         each("dev", 0, FAR, lambda t, i: send(own, r1.at[pl.ds(i, 1), :], S_R1 + it, "dev", t))
@@ -390,7 +412,6 @@
         await_bytes(r1.at[pl.ds(0, FAR), :], recv_sem.at[S_R1 + it])
         summed += scattered(r1, 0, FAR)
         slab_rhs = summed[0:HI] + summed[HI:]
-        coarse_b[...] = slab_rhs
         part = jnp.zeros((CK, FD), F32)
         for j in range(HI):
             part += coarse_p[:, FD * j : FD * (j + 1)] * slab_rhs[j : j + 1]
@@ -400,10 +421,13 @@
         row = jnp.where(lane1 == LO + 1, curve_part, row)
         if it:
             row = jnp.where(lane1 == LO + 2, cross_part, row)
-        r2[pl.ds(2 * g, 1), :] = row
-        r2[pl.ds(2 * g + 1, 1), :] = coarse_b[pl.ds(d, 1), :]
-        mine = r2.at[pl.ds(pl.multiple_of(2 * g, 2), 2), :]
-        send_all("grp", N_GRP, lambda t: mine, mine, S_R2 + it)
+        rows_of_all[pl.ds(me, 1), :] = row
+        mine = rows_of_all.at[pl.ds(me, 1), :]
+        send_everywhere(mine, S_R2 + it)
+        here = pl.ds(pl.multiple_of(HI * g, HI), HI)
+        rhs_of_all[here, :] = slab_rhs
+        own_rhs = rhs_of_all.at[here, :]
+        send_all("grp", N_GRP, lambda t: own_rhs, own_rhs, S_R3 + it)
 
         if it == 0:
             columns = table.T[0:CK]
@@ -440,22 +464,6 @@
                 gather_hi[rows, :] = jnp.where(high == lane_f, 1.0, 0.0).astype(BF16)
                 gather_lo[rows, :] = jnp.where(m - LO * high == lane_f, 1.0, 0.0)
 
-        await_bytes(r2.at[pl.ds(0, 2 * (N_GRP - 1)), :], recv_sem.at[S_R2 + it])
-        pairs = r2[...]
-        even = lax.rem(iota((2 * N_GRP, FD), 0), 2) == 0
-        sol_row = jnp.sum(jnp.where(even, pairs, 0.0), axis=0, keepdims=True)
-        rhs_row = jnp.sum(jnp.where(even, 0.0, pairs), axis=0, keepdims=True)
-        row = jnp.where(
-            lane1 == LO + 3, jnp.sum(sol_row * rhs_row, axis=1, keepdims=True), sol_row
-        )
-        if it:
-            row = jnp.where(
-                lane1 == LO + 4, jnp.sum(sol_row * coarse_dir, axis=1, keepdims=True), row
-            )
-        r3[pl.ds(d, 1), :] = row
-        own3 = r3.at[pl.ds(d, 1), :]
-        send_all("dev", N_DEV, lambda t: own3, own3, S_R3 + it)
-
         await_fields(buf, recv_sem, S_F + it)
         local_jump = jump_sign * (response - pick_rows(opposite_hot, buf[...]))
         if it == 0:
@@ -483,11 +491,17 @@
                         -jump_sign[r : r + 1] * beyond[f][KC * s : KC * (s + 1)]
                     )
 
-        await_bytes(r3.at[pl.ds(0, N_DEV - 1), :], recv_sem.at[S_R3 + it])
-        coarse_sol = r3[...]
+        await_bytes(rhs_of_all.at[pl.ds(0, HI * (N_GRP - 1)), :], recv_sem.at[S_R3 + it])
+        coarse_rhs = rhs_of_all[0:HI, :]
+        for k in range(1, N_GRP):
+            coarse_rhs += rhs_of_all[HI * k : HI * (k + 1), :]
+        await_bytes(rows_of_all.at[pl.ds(0, N_DEV * N_GRP - 1), :], recv_sem.at[S_R2 + it])
+        coarse_sol = rows_of_all[0:N_DEV, :]
+        for k in range(1, N_GRP):
+            coarse_sol += rows_of_all[N_DEV * k : N_DEV * (k + 1), :]
         sums = jnp.sum(coarse_sol, axis=0, keepdims=True)
         norm_now = sums[:, LO : LO + 1]
-        curve = sums[:, LO + 1 : LO + 2] + sums[:, LO + 3 : LO + 4]
+        curve = sums[:, LO + 1 : LO + 2] + total(coarse_sol * coarse_rhs)
         padded = jnp.concatenate([coarse_sol, jnp.zeros((FD - HI, FD), F32)], axis=0)
         at_corner = []
         sol_parts = split(padded, 2)
@@ -506,15 +520,15 @@
         image = local_jump + target[...]
 
         if it == 0:
-            direction, image_dir, local_dir, coarse_dir = scaled, image, response, rhs_row
+            direction, image_dir, local_dir, coarse_dir = scaled, image, response, coarse_rhs
         else:
             ratio = norm_now / norm_before
-            cross = sums[:, LO + 2 : LO + 3] + 2.0 * sums[:, LO + 4 : LO + 5]
+            cross = sums[:, LO + 2 : LO + 3] + 2.0 * total(coarse_sol * coarse_dir)
             curve = curve + ratio * cross + ratio * ratio * curve_before
             direction = scaled + ratio * direction
             image_dir = image + ratio * image_dir
             local_dir = response + ratio * local_dir
-            coarse_dir = rhs_row + ratio * coarse_dir
+            coarse_dir = coarse_rhs + ratio * coarse_dir
         step = norm_now / curve
         norm_before, curve_before = norm_now, curve
         result = result + step * direction
@@ -547,8 +561,8 @@
             vmem(FD, FD), vmem(FD, FD), vmem(256, FD), vmem(256, FD), vmem(2 * CK, FD), vmem(2, CK, FD),
             vmem(FACES, CK, FD), vmem(FACES, CK, FD),
             vmem(HI, HI * FD), pltpu.VMEM((HI * FD, FD), BF16),
-            pltpu.VMEM((7 * CK, FD), BF16), vmem(7 * CK, FD), vmem(FD, FD), vmem(HI, FD), vmem(FD, ROWS * FD), pltpu.VMEM((2 * HI, HI * FD), BF16),
-            vmem(ITERS, N_DEV, FD), vmem(ITERS, 2 * N_GRP, FD), vmem(ITERS, N_DEV, FD),
+            pltpu.VMEM((7 * CK, FD), BF16), vmem(7 * CK, FD), vmem(FD, FD), vmem(FD, ROWS * FD), pltpu.VMEM((2 * HI, HI * FD), BF16),
+            vmem(ITERS, N_DEV, FD), vmem(ITERS, N_DEV * N_GRP, FD), vmem(ITERS, HI * N_GRP, FD),
             pltpu.SemaphoreType.DMA((14,)),
             pltpu.SemaphoreType.DMA((21,)),
             pltpu.SemaphoreType.DMA((21,)),

time: 71 us -> 66 us (0.930)
  Pallas kernels: 68.8 us -> 63.8 us
    pallas_call x1, Pallas kernels: 68.8 us -> 63.8 us  [per_device(): pl.pallas_call(kernel, out_shape=field, in_specs=[pl.BlockSpec(memory_spa...]
where the time goes in v4:
time: 66 us; the launch traced here: 65.7 us
  Pallas kernels  63.8 us (97%)
  local copies, waits for them, and re-layouts  1.33 us (2%)
    pallas_call x1, Pallas kernels, per_device(): pl.pallas_call(kernel, out_shape=field, in_specs=[pl.BlockSpec(memory_spa...  63.8 us
    squeeze x1, local copies, waits for them, and re-layouts, per_device(): return (both[0], both[1])  1.33 us

profile of v4, /device:TPU:1, one launch (start us, length us, event | category | flops | bytes accessed | tf_op | source)
XLA Modules:
  0.0 65.7 jit_solution(9304370303141860926)
XLA Ops:
  0.6 63.8 %shard_map.95 = f32[2,4,768]{2,1,0:T(4,128)} custom-call(f32[4,768]{1,0:T(4,128)} %gap_hbm.1, f32[4,768]{1,0:T(4,128)} %wgt_hbm.1, s32[4,4]{1,0:T(4,128)} %links_hbm.1, s32[4,4]{1,0:T(4,128)} %lens_hbm.1, f32[4,768,768]{2,1,0:T(8,128)} %schur_hbm.1, s32[4,24]{1,0:T(4,128)} %map_hbm.1, f32[4,24,768]{2,1,0:T(8,128)} %coup_hbm.1, f32[96,3072]{1,0:T(8,128)} %coarse_hbm.1), custom_call_target="tpu_custom_call" | custom-call | tf_op jit(solution)/shard_map/pallas_call | solution.py:548
  64.4 1.3 %slice_bitcast_fusion = (f32[4,768]{1,0:T(4,128)}, f32[4,768]{1,0:T(4,128)}) fusion(f32[2,4,768]{2,1,0:T(4,128)} %shard_map.95), kind=kLoop, calls=%fused_computation | loop fusion | bytes 49152 | tf_op jit(solution)/shard_map/squeeze | solution.py:574

commit v5 on v4

--- a/solution.py
+++ b/solution.py
@@ -47,8 +47,8 @@
 
 
 def lane_sums(x):
-    ones = jnp.ones((8, x.shape[1]), BF16)
-    return sum(dot_nt(ones, part) for part in split(x, 2))[0:1]
+    ones = jnp.ones((8, 2 * x.shape[1]), BF16)
+    return dot_nt(ones, jnp.concatenate(split(x, 2), axis=1))[0:1]
 
 
 def total(x):
@@ -461,7 +461,8 @@
             for i, m in enumerate(maps):
                 high = jnp.floor((m + 0.5) * (1.0 / LO))
                 rows = slice(CK * i, CK * (i + 1))
-                gather_hi[rows, :] = jnp.where(high == lane_f, 1.0, 0.0).astype(BF16)
+                twice = (high == lane_f) | (high + HI == lane_f) | (high + 2 * HI == lane_f)
+                gather_hi[rows, :] = jnp.where(twice, 1.0, 0.0).astype(BF16)
                 gather_lo[rows, :] = jnp.where(m - LO * high == lane_f, 1.0, 0.0)
 
         await_fields(buf, recv_sem, S_F + it)
@@ -502,13 +503,13 @@
         sums = jnp.sum(coarse_sol, axis=0, keepdims=True)
         norm_now = sums[:, LO : LO + 1]
         curve = sums[:, LO + 1 : LO + 2] + total(coarse_sol * coarse_rhs)
-        padded = jnp.concatenate([coarse_sol, jnp.zeros((FD - HI, FD), F32)], axis=0)
+        sol_parts = jnp.concatenate(
+            split(coarse_sol, 3) + [jnp.zeros((FD - 3 * HI, FD), BF16)], axis=0
+        )
         at_corner = []
-        sol_parts = split(padded, 2)
         for i in range(7):
             rows = slice(CK * i, CK * (i + 1))
-            hot = gather_hi[rows, :]
-            got = sum(dot(hot, p) for p in sol_parts) * gather_lo[rows, :]
+            got = dot(gather_hi[rows, :], sol_parts) * gather_lo[rows, :]
             at_corner.append(jnp.sum(got, axis=1, keepdims=True))
         for f in range(FACES):
             both = own_w[f] * at_corner[0] + next_w[f] * at_corner[1 + f]

time: 66 us -> 65.6 us (level)
  no operation moved by 1% of the time
where the time goes in v5:
time: 65.6 us; the launch traced here: 65.3 us
  Pallas kernels  63.3 us (96%)
  local copies, waits for them, and re-layouts  1.33 us (2%)
    pallas_call x1, Pallas kernels, per_device(): pl.pallas_call(kernel, out_shape=field, in_specs=[pl.BlockSpec(memory_spa...  63.3 us
    squeeze x1, local copies, waits for them, and re-layouts, per_device(): return (both[0], both[1])  1.33 us

profile of v5, /device:TPU:1, one launch (start us, length us, event | category | flops | bytes accessed | tf_op | source)
XLA Modules:
  0.0 65.3 jit_solution(5844223753146550601)
XLA Ops:
  0.6 63.3 %shard_map.95 = f32[2,4,768]{2,1,0:T(4,128)} custom-call(f32[4,768]{1,0:T(4,128)} %gap_hbm.1, f32[4,768]{1,0:T(4,128)} %wgt_hbm.1, s32[4,4]{1,0:T(4,128)} %links_hbm.1, s32[4,4]{1,0:T(4,128)} %lens_hbm.1, f32[4,768,768]{2,1,0:T(8,128)} %schur_hbm.1, s32[4,24]{1,0:T(4,128)} %map_hbm.1, f32[4,24,768]{2,1,0:T(8,128)} %coup_hbm.1, f32[96,3072]{1,0:T(8,128)} %coarse_hbm.1), custom_call_target="tpu_custom_call" | custom-call | tf_op jit(solution)/shard_map/pallas_call | solution.py:549
  64.0 1.3 %slice_bitcast_fusion = (f32[4,768]{1,0:T(4,128)}, f32[4,768]{1,0:T(4,128)}) fusion(f32[2,4,768]{2,1,0:T(4,128)} %shard_map.95), kind=kLoop, calls=%fused_computation | loop fusion | bytes 49152 | tf_op jit(solution)/shard_map/squeeze | solution.py:575
